TPU v7x, 256 devices: a whole 4x4x8 slice. The times are simulated.
256 devices in a mesh: acq: 4 (over x), tile: 64 (over z, y, core).
Axes of the slice: x: 4, y: 4, z: 8, core: 2. Of those that a mesh axis runs over, the one named last changes fastest.
Arguments:
- slc: bfloat16 [16, 2, 8192, 1280], P('acq', None, 'tile')
- match: int32 [2, 16], replicated, may hold values from 0 to 3, as said below
- dest: int32 [64, 16, 32, 1], P('tile', 'acq'), may hold values from 0 to 3; in each aligned block of 128 rows (0 to 127, 128 to 255, ..., all dimensions but the last counted through in order) at most 64 rows name the same one
- coherent: int32 [64, 16, 32], P('tile', 'acq'), may hold values 0 or 1
Outputs:
- received: bfloat16 [64, 1024, 2, 128], P('tile', 'acq')
Inputs may be any that keep to these rules, and one draw needn't show every extreme that they name: `match`: within each round, the entries of each aligned run of 4 acquisitions are a permutation of 0 to 3. `dest`: among the 128 rows of one device, at most 64 name the same owner.
All inputs are finite; a program needn't handle non-finite values. No bound on the sum of `coherent` on one device may be relied on, other than what follows from the above.
Results may differ from a plain program's by a relative error of at most 0.001.
Values may be sent and summed in bfloat16 or wider, within the bound.
No kernel may reach another device: no remote copies, remote signals or barrier semaphores. Data moves between devices by JAX's collectives and lax.ppermute only.
A program may use at most 128 MiB of HBM per device.

v0:
```python
import jax
import jax.numpy as jnp
from jax import lax
from jax.sharding import PartitionSpec as P

PATCH = 32
LOOK_L = 4
LOOK_S = 20
BLOCK_ROWS = 4
ROUNDS = 2
power_floor = 0.25
energy_eps = 1e-06


def swapped(x, axis, stride):
    return lax.ppermute(x, axis, [(i, i ^ 1 << stride) for i in range(lax.axis_size(axis))])


def dft_tables():
    counter = jnp.arange(PATCH)
    phase = counter[:, None] * counter[None, :] % PATCH
    angle = phase.astype(jnp.float32) * (2.0 * 3.141592653589793 / PATCH)
    return (jnp.cos(angle), jnp.sin(angle))


def along_axes(real_part, imag_part, cosine, sine_tab, sign, form):
    hold = lax.Precision.HIGHEST
    c_real = jnp.einsum(form, cosine, real_part, precision=hold)
    c_imag = jnp.einsum(form, cosine, imag_part, precision=hold)
    s_real = jnp.einsum(form, sine_tab, real_part, precision=hold)
    s_imag = jnp.einsum(form, sine_tab, imag_part, precision=hold)
    return (c_real - sign * s_imag, c_imag + sign * s_real)


def transform(real_part, imag_part, cosine, sine_tab, sign):
    real_part, imag_part = along_axes(
        real_part, imag_part, cosine, sine_tab, sign, "jk,aPkQl->aPjQl"
    )
    return along_axes(real_part, imag_part, cosine, sine_tab, sign, "lm,aPkQm->aPkQl")


def cross_looks(left, right, picks):
    acq_dev, _, line_count, sample_count = left.shape
    other = jnp.take(right, picks, axis=0)
    own_real = left[:, 0].astype(jnp.float32)
    own_imag = left[:, 1].astype(jnp.float32)
    other_real = other[:, 0].astype(jnp.float32)
    other_imag = other[:, 1].astype(jnp.float32)
    real_part = own_real * other_real + own_imag * other_imag
    imag_part = own_imag * other_real - own_real * other_imag
    stacked = jnp.stack([real_part, imag_part], axis=1)
    stacked = stacked.reshape(
        acq_dev, 2, line_count // LOOK_L, LOOK_L, sample_count // LOOK_S, LOOK_S
    )
    return jnp.sum(stacked, axis=(3, 5)) / (LOOK_L * LOOK_S)


def shards(slc, match, dest, coherent):
    acq_dev, _, lines_dev, samples_dev = slc.shape
    n_acq = lax.axis_size("acq")
    n_tile = lax.axis_size("tile")
    far_bit = n_acq.bit_length() - 2
    grid_count = lines_dev * n_tile // LOOK_L * (samples_dev // LOOK_S)
    patch_rows = lines_dev // LOOK_L // PATCH
    patch_cols = samples_dev // LOOK_S // PATCH
    cosine, sine_tab = dft_tables()
    my_group = lax.axis_index("acq")

    def swap_tiles(tiles, round_number):
        if round_number == 0:
            return swapped(tiles, "acq", 0)
        return swapped(tiles, "acq", far_bit)

    order_list = [0, 1]
    looked_all = {}
    filtered_all = {}
    for round_number in order_list:
        own_match = lax.dynamic_slice_in_dim(match[round_number], my_group * acq_dev, acq_dev)
        group_tiles = swap_tiles(slc, round_number)
        looked_all[round_number] = cross_looks(slc, group_tiles, own_match)
        local_looked = looked_all[round_number]
        total = lax.psum(
            jnp.sum(local_looked[:, 0] ** 2 + local_looked[:, 1] ** 2, axis=(1, 2)), "tile"
        )
        energy = total / grid_count + energy_eps
        looked = looked_all[round_number]
        shape_six = (acq_dev, patch_rows, PATCH, patch_cols, PATCH)
        real_part = looked[:, 0].reshape(shape_six)
        imag_part = looked[:, 1].reshape(shape_six)
        spec_real, spec_imag = transform(real_part, imag_part, cosine, sine_tab, -1.0)
        scale = energy[:, None, None, None, None]
        power = (spec_real**2 + spec_imag**2) / (PATCH * PATCH * scale)
        weight = (power + power_floor) ** 0.25
        back_real, back_imag = transform(
            weight * spec_real, weight * spec_imag, cosine, sine_tab, 1.0
        )
        norm_factor = 1.0 / (PATCH * PATCH * jnp.sqrt(scale))
        parts = jnp.stack([back_real * norm_factor, back_imag * norm_factor], axis=-1)
        parts = parts.reshape(
            acq_dev, patch_rows, PATCH // BLOCK_ROWS, BLOCK_ROWS, patch_cols, PATCH, 2
        )
        parts = jnp.transpose(parts, (0, 1, 2, 4, 6, 3, 5))
        filtered_all[round_number] = parts.reshape(
            acq_dev, patch_rows * (PATCH // BLOCK_ROWS) * patch_cols, 2, BLOCK_ROWS * PATCH
        )
    stacked = jnp.stack([filtered_all[round_number] for round_number in range(ROUNDS)], axis=1)
    block_len = BLOCK_ROWS * PATCH
    rows_dev = stacked.shape[0] * stacked.shape[1] * stacked.shape[2]
    cap_rows = max(3, 2 * ((rows_dev + n_acq - 1) // n_acq))
    stacked = stacked.reshape(rows_dev, 2, block_len)
    mask_rows = coherent.reshape(rows_dev).astype(jnp.float32)
    value = (stacked * mask_rows[:, None, None]).astype(jnp.bfloat16)
    owner = dest.reshape(rows_dev)
    onehot = (owner[:, None] == jnp.arange(n_acq)).astype(jnp.int32)
    rank = jnp.sum((jnp.cumsum(onehot, axis=0) - onehot) * onehot, axis=1)
    hits = (onehot[:, :, None] == 1) & (rank[:, None, None] == jnp.arange(cap_rows)[None, None, :])
    select = hits.astype(jnp.bfloat16).reshape(rows_dev, n_acq * cap_rows)
    outgoing = jnp.einsum("ks,kcp->scp", select, value, preferred_element_type=jnp.float32).astype(
        jnp.bfloat16
    )
    incoming = lax.all_to_all(outgoing, "acq", split_axis=0, concat_axis=0, tiled=True)
    return incoming[None]


def solution(mesh):
    return jax.shard_map(
        shards,
        mesh=mesh,
        in_specs=(
            P("acq", None, "tile", None),
            P(),
            P("tile", "acq", None, None),
            P("tile", "acq", None),
        ),
        out_specs=P("tile", "acq", None, None),
        check_vma=False,
    )
```

profile of v0, /device:TPU:2, one launch (start us, length us, event | category | flops | bytes accessed | tf_op | source)
XLA Modules:
  0.0 392.0 jit_solution(11845834372850043596)
XLA Ops:
  0.0 2.1 collective-permute-start.1
  2.1 1.4 collective-permute-start
  3.6 0.7 convert_element_type.142
  4.8 1.3 reduce.5
  6.6 0.8 fusion.240
  7.8 53.8 %collective-permute-done.1 = bf16[4,2,128,1280]{3,2,1,0:T(8,128)(2,1)} collective-permute-done((bf16[4,2,128,1280]{3,2,1,0:T(8,128)(2,1)}, bf16[4,2,128,1280]{3,2,1,0:T(8,128)(2,1)}, u32[]{:S(2)}, u32[]{:S(2)}) %collective-permute-start.1) | collective-permute-done | bytes 2621472 | tf_op jit(solution)/shard_map/ppermute | solution.py:16
  61.6 2.5 gather_fusion.1
  64.0 1.8 broadcast_select_fusion
  65.9 50.8 %collective-permute-done = bf16[4,2,128,1280]{3,2,1,0:T(8,128)(2,1)} collective-permute-done((bf16[4,2,128,1280]{3,2,1,0:T(8,128)(2,1)}, bf16[4,2,128,1280]{3,2,1,0:T(8,128)(2,1)}, u32[]{:S(2)}, u32[]{:S(2)}) %collective-permute-start) | collective-permute-done | bytes 2621472 | tf_op jit(solution)/shard_map/ppermute | solution.py:16
  116.6 2.5 gather_fusion
  119.4 1.4 copy-done
  120.8 0.8 copy-done.1
  121.6 4.0 %fusion = (f32[4,1,128,1280]{3,2,1,0:T(8,128)}, f32[4,1,128,1280]{3,2,1,0:T(8,128)}, f32[4,1,128,1280]{3,2,1,0:T(8,128)S(1)}, f32[4,1,128,1280]{3,2,1,0:T(8,128)}) fusion(bf16[4,2,128,1280]{3,2,1,0:T(8,128)(2,1)S(1)} %broadcast_select_fusion.1, bf16[4,2,128,1280]{3,2,1,0:T(8,128)(2,1)S(1)} %copy-done.1, bf16[4,2,128,1280]{3,2,1,0:T(8,128)(2,1)S(1)} %copy-done), kind=kLoop, calls=%fused_computation.12 | loop fusion | flops 11796480 | bytes 18350080 | tf_op jit(solution)/shard_map/add | solution.py:49
  125.6 21.7 %stack.39 = f32[4,1,32,4,64,20]{5,4,3,2,0,1:T(8,128)} reshape(f32[4,1,128,1280]{3,2,1,0:T(8,128)} %get-tuple-element.12) | data formatting | bytes 5242880 | tf_op jit(solution)/shard_map/stack | solution.py:51
  147.3 21.7 %stack.40 = f32[4,1,32,4,64,20]{5,4,3,2,0,1:T(8,128)} reshape(f32[4,1,128,1280]{3,2,1,0:T(8,128)} %get-tuple-element.13) | data formatting | bytes 5242880 | tf_op jit(solution)/shard_map/stack | solution.py:51
  168.9 12.7 %maximum_reduce_fusion = f32[4,2,32,64]{3,2,0,1:T(8,128)S(1)} fusion(f32[4,1,32,4,64,20]{5,4,3,2,0,1:T(8,128)} %stack.40, f32[4,1,32,4,64,20]{5,4,3,2,0,1:T(8,128)} %stack.39), kind=kLoop, calls=%fused_computation.2 | loop fusion | flops 2605056 | bytes 5308416 | tf_op jit(solution)/shard_map/reduce_sum | solution.py:55
  185.0 21.7 %stack.45 = f32[4,1,32,4,64,20]{5,4,3,2,0,1:T(8,128)} reshape(f32[4,1,128,1280]{3,2,1,0:T(8,128)} %get-tuple-element.17) | data formatting | bytes 5242880 | tf_op jit(solution)/shard_map/stack | solution.py:51
  206.7 20.9 %stack.46 = f32[4,1,32,4,64,20]{5,4,3,2,0,1:T(8,128)} reshape(f32[4,1,128,1280]{3,2,1,0:T(8,128)S(1)} %get-tuple-element.16) | data formatting | bytes 5242880 | tf_op jit(solution)/shard_map/stack | solution.py:51
  227.6 12.7 %maximum_reduce_fusion.1 = f32[4,2,32,64]{3,2,0,1:T(8,128)S(1)} fusion(f32[4,1,32,4,64,20]{5,4,3,2,0,1:T(8,128)} %stack.46, f32[4,1,32,4,64,20]{5,4,3,2,0,1:T(8,128)} %stack.45), kind=kLoop, calls=%fused_computation.3 | loop fusion | flops 2605056 | bytes 5308416 | tf_op jit(solution)/shard_map/reduce_sum | solution.py:55
  240.5 131.1 %all-reduce = (f32[4]{0:T(128)S(1)}, f32[4]{0:T(128)S(1)}) all-reduce(f32[4]{0:T(128)S(1)} %get-tuple-element.21, f32[4]{0:T(128)S(1)} %get-tuple-element.19), channel_id=1, replica_groups=mesh['acq'=4,'tile'=64] {'tile'}, use_global_device_ids=true, to_apply=%region_7.9 | all-reduce | flops 8 | bytes 64 | tf_op jit(solution)/shard_map/psum | solution.py:82
  376.9 0.5 fusion.9
  380.7 0.5 fusion.4
  383.1 8.2 %all_to_all.5 = bf16[256,2,128]{2,1,0:T(2,128)(2,1)S(1)} all-to-all(bf16[256,2,128]{2,1,0:T(2,128)(2,1)S(1)} %copy.171), channel_id=1, replica_groups=mesh['acq'=4,'tile'=64] {'acq'}, dimensions={0} | all-to-all | bytes 262144 | tf_op jit(solution)/shard_map/all_to_all | solution.py:121
  391.3 0.7 copy.205
  (64 shorter events, 15.4 us)
Async XLA Ops:
  0.0 61.6 %collective-permute-start.1 = (bf16[4,2,128,1280]{3,2,1,0:T(8,128)(2,1)}, bf16[4,2,128,1280]{3,2,1,0:T(8,128)(2,1)}, u32[]{:S(2)}, u32[]{:S(2)}) collective-permute-start(bf16[4,2,128,1280]{3,2,1,0:T(8,128)(2,1)} %param.6), channel_id=1, source_target_pairs={{0,128},{64,192},{128,0},{192,64},{1,129},{65,193},{129,1},{193,65... | collective-permute-start | bytes 7864328 | tf_op jit(solution)/shard_map/ppermute | solution.py:16
  2.1 114.5 %collective-permute-start = (bf16[4,2,128,1280]{3,2,1,0:T(8,128)(2,1)}, bf16[4,2,128,1280]{3,2,1,0:T(8,128)(2,1)}, u32[]{:S(2)}, u32[]{:S(2)}) collective-permute-start(bf16[4,2,128,1280]{3,2,1,0:T(8,128)(2,1)} %param.6), channel_id=1, source_target_pairs={{0,64},{64,0},{128,192},{192,128},{1,65},{65,1},{129,193},{193,129... | collective-permute-start | bytes 7864328 | tf_op jit(solution)/shard_map/ppermute | solution.py:16
  119.1 1.7 copy-start
  119.1 2.5 copy-start.1
where the time goes:
time: 392 us
  blocking collectives  139 us (35%)
  waiting for transfers between devices  105 us (27%)
  local copies, waits for them, and re-layouts  96 us (24%)
  other arithmetic  34.8 us (9%)
  matrix products  13.3 us (3%)
    psum x1, blocking collectives, shards(): lax.psum(jnp.sum(local_looked[:, 0] ** 2 + local_looked[:, 1] ** 2, axis=...  131 us
    ppermute x2, waiting for transfers between devices, swapped(): lax.ppermute(x, axis, [(i, i ^ 1 << stride) for i in range(lax.axis_size(...  105 us
    another operation x4, local copies, waits for them, and re-layouts, cross_looks(): stacked = jnp.stack([real_part, imag_part], axis=1)  85.9 us
    reduce_sum x2, other arithmetic, cross_looks(): return jnp.sum(stacked, axis=(3, 5)) / (LOOK_L * LOOK_S)  25.5 us
    all_to_all x1, blocking collectives, shards(): lax.all_to_all(outgoing, 'acq', split_axis=0, concat_axis=0, tiled=True)  8.18 us
  transfers between devices with their start and end apart: 2, of which 2 were waited for; matrix products, arithmetic and copies ran while one was open for 2% of the time, Pallas kernels for 0%

commit v1 on v0

--- a/solution.py
+++ b/solution.py
@@ -10,6 +10,28 @@
 ROUNDS = 2
 power_floor = 0.25
 energy_eps = 1e-06
+
+
+def in_blocks(value, dim, size):
+    before, after = (value.shape[:dim], value.shape[dim + 1 :])
+    return jnp.moveaxis(value.reshape(*before, size, -1, *after), dim, 0)
+
+
+def joined_along(blocks, dim):
+    blocks = jnp.moveaxis(blocks, 0, dim)
+    shape = blocks.shape
+    return blocks.reshape(*shape[:dim], shape[dim] * shape[dim + 1], *shape[dim + 2 :])
+
+
+def sent_to_each(value, axis, split_dim, concat_dim):
+    length, index = (lax.axis_size(axis), lax.axis_index(axis))
+    pieces = in_blocks(value, split_dim, length)
+    finished = [pieces[index]]
+    for step in range(1, length):
+        sent = pieces[(index + step) % length]
+        finished.append(lax.ppermute(sent, axis, [(i, (i + step) % length) for i in range(length)]))
+    pieces = jnp.stack(finished)[(index - jnp.arange(length)) % length]
+    return joined_along(pieces, concat_dim)
 
 
 def swapped(x, axis, stride):
@@ -118,7 +140,7 @@
     outgoing = jnp.einsum("ks,kcp->scp", select, value, preferred_element_type=jnp.float32).astype(
         jnp.bfloat16
     )
-    incoming = lax.all_to_all(outgoing, "acq", split_axis=0, concat_axis=0, tiled=True)
+    incoming = sent_to_each(outgoing, "acq", 0, 0)
     return incoming[None]
 
 

time: 392 us -> 392 us (level)
  blocking collectives: 139 us -> 131 us
    all_to_all x1 -> x0, blocking collectives: 8.18 us -> none  [shards(): lax.all_to_all(outgoing, 'acq', split_axis=0, concat_axis=0, tiled=True)]
  transfers between devices with their start and end apart: 2 -> 5, of which waited for: 2 -> 5; matrix products, arithmetic and copies ran while one was open for 2% -> 2% of each run, Pallas kernels for 0% -> 0%
where the time goes in v1:
time: 392 us; the launch traced here: 391 us
  blocking collectives  131 us (33%)
  waiting for transfers between devices  108 us (28%)
  local copies, waits for them, and re-layouts  96.6 us (25%)
  other arithmetic  34.8 us (9%)
  matrix products  13.3 us (3%)
  starting transfers between devices  6.32 us (2%)
    psum x1, blocking collectives, shards(): lax.psum(jnp.sum(local_looked[:, 0] ** 2 + local_looked[:, 1] ** 2, axis=...  131 us
    ppermute x2, waiting for transfers between devices, swapped(): lax.ppermute(x, axis, [(i, i ^ 1 << stride) for i in range(lax.axis_size(...  105 us
    another operation x4, local copies, waits for them, and re-layouts, cross_looks(): stacked = jnp.stack([real_part, imag_part], axis=1)  85.9 us
    reduce_sum x2, other arithmetic, cross_looks(): return jnp.sum(stacked, axis=(3, 5)) / (LOOK_L * LOOK_S)  25.5 us
  transfers between devices with their start and end apart: 5, of which 5 were waited for; matrix products, arithmetic and copies ran while one was open for 2% of the time, Pallas kernels for 0%

profile of v1, /device:TPU:2, one launch (start us, length us, event | category | flops | bytes accessed | tf_op | source)
XLA Modules:
  0.0 391.0 jit_solution(140049365928203287)
XLA Ops:
  0.0 2.1 collective-permute-start.1
  2.1 1.4 collective-permute-start
  3.6 0.7 convert_element_type.142
  4.8 1.3 reduce.5
  6.7 0.8 fusion.244
  7.8 53.8 %collective-permute-done.1 = bf16[4,2,128,1280]{3,2,1,0:T(8,128)(2,1)} collective-permute-done((bf16[4,2,128,1280]{3,2,1,0:T(8,128)(2,1)}, bf16[4,2,128,1280]{3,2,1,0:T(8,128)(2,1)}, u32[]{:S(2)}, u32[]{:S(2)}) %collective-permute-start.1) | collective-permute-done | bytes 2621472 | tf_op jit(solution)/shard_map/ppermute | solution.py:38
  61.6 2.5 gather_fusion.2
  64.0 1.8 broadcast_select_fusion
  65.9 50.8 %collective-permute-done = bf16[4,2,128,1280]{3,2,1,0:T(8,128)(2,1)} collective-permute-done((bf16[4,2,128,1280]{3,2,1,0:T(8,128)(2,1)}, bf16[4,2,128,1280]{3,2,1,0:T(8,128)(2,1)}, u32[]{:S(2)}, u32[]{:S(2)}) %collective-permute-start) | collective-permute-done | bytes 2621472 | tf_op jit(solution)/shard_map/ppermute | solution.py:38
  116.6 2.5 gather_fusion.1
  119.4 1.4 copy-done
  120.8 0.8 copy-done.1
  121.6 4.0 %fusion = (f32[4,1,128,1280]{3,2,1,0:T(8,128)}, f32[4,1,128,1280]{3,2,1,0:T(8,128)}, f32[4,1,128,1280]{3,2,1,0:T(8,128)S(1)}, f32[4,1,128,1280]{3,2,1,0:T(8,128)}) fusion(bf16[4,2,128,1280]{3,2,1,0:T(8,128)(2,1)S(1)} %broadcast_select_fusion.1, bf16[4,2,128,1280]{3,2,1,0:T(8,128)(2,1)S(1)} %copy-done.1, bf16[4,2,128,1280]{3,2,1,0:T(8,128)(2,1)S(1)} %copy-done), kind=kLoop, calls=%fused_computation.13 | loop fusion | flops 11796480 | bytes 18350080 | tf_op jit(solution)/shard_map/add | solution.py:71
  125.6 21.7 %stack.51 = f32[4,1,32,4,64,20]{5,4,3,2,0,1:T(8,128)} reshape(f32[4,1,128,1280]{3,2,1,0:T(8,128)} %get-tuple-element.12) | data formatting | bytes 5242880 | tf_op jit(solution)/shard_map/stack | solution.py:73
  147.3 21.7 %stack.52 = f32[4,1,32,4,64,20]{5,4,3,2,0,1:T(8,128)} reshape(f32[4,1,128,1280]{3,2,1,0:T(8,128)} %get-tuple-element.13) | data formatting | bytes 5242880 | tf_op jit(solution)/shard_map/stack | solution.py:73
  168.9 12.7 %maximum_reduce_fusion = f32[4,2,32,64]{3,2,0,1:T(8,128)S(1)} fusion(f32[4,1,32,4,64,20]{5,4,3,2,0,1:T(8,128)} %stack.52, f32[4,1,32,4,64,20]{5,4,3,2,0,1:T(8,128)} %stack.51), kind=kLoop, calls=%fused_computation.3 | loop fusion | flops 2605056 | bytes 5308416 | tf_op jit(solution)/shard_map/reduce_sum | solution.py:77
  185.0 21.7 %stack.57 = f32[4,1,32,4,64,20]{5,4,3,2,0,1:T(8,128)} reshape(f32[4,1,128,1280]{3,2,1,0:T(8,128)} %get-tuple-element.17) | data formatting | bytes 5242880 | tf_op jit(solution)/shard_map/stack | solution.py:73
  206.7 20.9 %stack.58 = f32[4,1,32,4,64,20]{5,4,3,2,0,1:T(8,128)} reshape(f32[4,1,128,1280]{3,2,1,0:T(8,128)S(1)} %get-tuple-element.16) | data formatting | bytes 5242880 | tf_op jit(solution)/shard_map/stack | solution.py:73
  227.6 12.7 %maximum_reduce_fusion.1 = f32[4,2,32,64]{3,2,0,1:T(8,128)S(1)} fusion(f32[4,1,32,4,64,20]{5,4,3,2,0,1:T(8,128)} %stack.58, f32[4,1,32,4,64,20]{5,4,3,2,0,1:T(8,128)} %stack.57), kind=kLoop, calls=%fused_computation.4 | loop fusion | flops 2605056 | bytes 5308416 | tf_op jit(solution)/shard_map/reduce_sum | solution.py:77
  240.5 131.1 %all-reduce = (f32[4]{0:T(128)S(1)}, f32[4]{0:T(128)S(1)}) all-reduce(f32[4]{0:T(128)S(1)} %get-tuple-element.25, f32[4]{0:T(128)S(1)} %get-tuple-element.23), channel_id=1, replica_groups=mesh['acq'=4,'tile'=64] {'tile'}, use_global_device_ids=true, to_apply=%region_7.9 | all-reduce | flops 8 | bytes 64 | tf_op jit(solution)/shard_map/psum | solution.py:104
  383.6 2.1 collective-permute-start.3
  385.8 1.2 collective-permute-done.2
  387.0 2.0 collective-permute-done.3
  390.3 0.8 copy.171
  (73 shorter events, 18.2 us)
Async XLA Ops:
  0.0 61.6 %collective-permute-start.1 = (bf16[4,2,128,1280]{3,2,1,0:T(8,128)(2,1)}, bf16[4,2,128,1280]{3,2,1,0:T(8,128)(2,1)}, u32[]{:S(2)}, u32[]{:S(2)}) collective-permute-start(bf16[4,2,128,1280]{3,2,1,0:T(8,128)(2,1)} %param.6), channel_id=1, source_target_pairs={{0,128},{64,192},{128,0},{192,64},{1,129},{65,193},{129,1},{193,65... | collective-permute-start | bytes 7864328 | tf_op jit(solution)/shard_map/ppermute | solution.py:38
  2.1 114.5 %collective-permute-start = (bf16[4,2,128,1280]{3,2,1,0:T(8,128)(2,1)}, bf16[4,2,128,1280]{3,2,1,0:T(8,128)(2,1)}, u32[]{:S(2)}, u32[]{:S(2)}) collective-permute-start(bf16[4,2,128,1280]{3,2,1,0:T(8,128)(2,1)} %param.6), channel_id=1, source_target_pairs={{0,64},{64,0},{128,192},{192,128},{1,65},{65,1},{129,193},{193,129... | collective-permute-start | bytes 7864328 | tf_op jit(solution)/shard_map/ppermute | solution.py:38
  119.1 1.7 copy-start
  119.1 2.5 copy-start.1
  383.0 4.0 %collective-permute-start.2 = (bf16[64,2,128]{2,0,1:T(8,128)(2,1)S(1)}, bf16[64,2,128]{2,0,1:T(8,128)(2,1)S(1)}, u32[]{:S(2)}, u32[]{:S(2)}) collective-permute-start(bf16[64,2,128]{2,0,1:T(8,128)(2,1)S(1)} %get-tuple-element.21), channel_id=1, source_target_pairs={{0,64},{64,128},{128,192},{192,0},{1,65},{65,129},{129,193},{193,1... | collective-permute-start | bytes 98312 | tf_op jit(solution)/shard_map/ppermute | solution.py:32
  383.6 5.4 %collective-permute-start.3 = (bf16[64,2,128]{2,0,1:T(8,128)(2,1)S(1)}, bf16[64,2,128]{2,0,1:T(8,128)(2,1)S(1)}, u32[]{:S(2)}, u32[]{:S(2)}) collective-permute-start(bf16[64,2,128]{2,0,1:T(8,128)(2,1)S(1)} %get-tuple-element.20), channel_id=1, source_target_pairs={{0,128},{64,192},{128,0},{192,64},{1,129},{65,193},{129,1},{193,65... | collective-permute-start | bytes 98312 | tf_op jit(solution)/shard_map/ppermute | solution.py:32
  385.7 3.9 %collective-permute-start.4 = (bf16[64,2,128]{2,0,1:T(8,128)(2,1)S(1)}, bf16[64,2,128]{2,0,1:T(8,128)(2,1)S(1)}, u32[]{:S(2)}, u32[]{:S(2)}) collective-permute-start(bf16[64,2,128]{2,0,1:T(8,128)(2,1)S(1)} %get-tuple-element.19), channel_id=1, source_target_pairs={{0,192},{64,0},{128,64},{192,128},{1,193},{65,1},{129,65},{193,129... | collective-permute-start | bytes 98312 | tf_op jit(solution)/shard_map/ppermute | solution.py:32
